TPU v7x, 32 devices: a whole 2x2x4 slice. The times are simulated.
32 devices in a mesh: pipe: 4 (over z), expert: 4 (over x, core), tensor: 2 (over y).
Axes of the slice: x: 2, y: 2, z: 4, core: 2. Of those that a mesh axis runs over, the one named last changes fastest.
Arguments:
- acts: bfloat16 [4, 4, 256, 1792], P('pipe', 'expert'), may hold values from -6 to 6
- hidden_grad: bfloat16 [4, 2, 256, 1024], P('pipe', None, None, 'tensor'), may hold values from -0.5 to 0.5
- counts: int32 [4, 2, 2], P('pipe'), may hold values from 32 to 128, as said below
- momentum: bfloat16 [4, 4, 1792, 1024], P('pipe', 'expert', 'tensor'), may hold values from -6 to 6
- act_grad: bfloat16 [4, 256, 7168], P('pipe', 'expert', 'tensor'), may hold values from -6 to 6
Outputs:
- new_momentum: bfloat16 [4, 4, 1792, 1024], P('pipe', 'expert', 'tensor')
- gram_rows: float32 [4, 4, 256, 1024], P('pipe', 'expert', 'tensor')
- received: bfloat16 [4, 256, 7168], P('pipe', 'expert', 'tensor')
Inputs may be any that keep to these rules, and one draw needn't show every extreme that they name: `counts`: in every section and expert, at least one micro-batch fills its block.
All inputs are finite; a program needn't handle non-finite values.
Results may differ from a plain program's by a relative error of at most 0.0065.
Values may be sent and summed in bfloat16 or wider, within the bound.
A program may use at most 64 MiB of HBM per device.

v0:
```python
import functools

import jax
import jax.numpy as jnp
from jax import lax
from jax.experimental import pallas as pl
from jax.experimental.pallas import tpu as pltpu
from jax.sharding import PartitionSpec as P

D = 3584
PANEL = 512
DECAY = 0.9
MESH = pl.DeviceIdType.MESH


def kernel(
    sections, ranks,
    acts, hidden, counts_in, momentum, act_grad,
    new_momentum, gram, received,
    counts, x_buf, g_own, m_buf, xt_buf, g_in, nt_buf, own, send1, recv1, send2, recv2,
    load_sem, shift_send, shift_recv,
    g_send, g_recv, f_send, f_recv, s1_send, s1_recv, s2_send, s2_recv,
):
    section = lax.axis_index("pipe")
    expert_rank = lax.axis_index("expert")
    rank = lax.axis_index("tensor")
    pair = expert_rank // 2
    half = expert_rank % 2
    partner = {"expert": expert_rank + 1 - 2 * half}
    row_count, features = x_buf.shape
    rows, hidden_units = new_momentum.shape
    q, wide = send1.shape[2:]
    per_rank = g_own.shape[1] // wide
    share = row_count // 2
    first, last = section == 0, section == sections - 1

    if features == rows:
        x_src = acts.at[0, 0, :, pl.ds(pl.multiple_of(rank * rows, 128), rows)]
    else:
        x_src = acts.at[0, 0]
    load_x = pltpu.make_async_copy(x_src, x_buf, load_sem.at[0])
    load_g = pltpu.make_async_copy(hidden.at[0, pair], g_own, load_sem.at[1])
    load_m = pltpu.make_async_copy(momentum.at[0, 0], m_buf, load_sem.at[2])
    load_counts = pltpu.make_async_copy(counts_in, counts, load_sem.at[3])
    load_g.start()

    barrier = pltpu.get_barrier_semaphore()
    pl.semaphore_signal(barrier, inc=1, device_id=partner, device_id_type=MESH)
    for k in range(1, ranks):
        pl.semaphore_signal(
            barrier, inc=1, device_id={"tensor": (rank + k) % ranks}, device_id_type=MESH
        )

    @pl.when(jnp.logical_not(first))
    def _():
        pl.semaphore_signal(barrier, inc=1, device_id={"pipe": section - 1}, device_id_type=MESH)

    @pl.when(jnp.logical_not(last))
    def _():
        pl.semaphore_signal(barrier, inc=1, device_id={"pipe": section + 1}, device_id_type=MESH)

    ends = jnp.where(first, 1, 0) + jnp.where(last, 1, 0)
    load_x.start()
    load_counts.start()
    load_m.start()
    load_g.wait()
    pl.semaphore_wait(barrier, ranks + 2 - ends)

    shift = pltpu.make_async_remote_copy(
        src_ref=act_grad,
        dst_ref=received,
        send_sem=shift_send,
        recv_sem=shift_recv,
        device_id={"pipe": section - 1},
        device_id_type=MESH,
    )

    def clear_dead_rows():
        row = lax.broadcasted_iota(jnp.int32, (row_count, 1), 0)
        micro = counts.shape[2]
        block = row_count // micro
        limit = jnp.zeros((row_count, 1), jnp.int32)
        for b in range(micro):
            inside = jnp.logical_and(row >= b * block, row < (b + 1) * block)
            limit = jnp.where(inside, counts[0, pair, b] + b * block, limit)
        live = jnp.where(row < limit, 1.0, 0.0).astype(jnp.float32)
        masked = (x_buf[...].astype(jnp.float32) * live).astype(jnp.bfloat16)
        xt_buf[...] = masked.T

    def own_share(which):
        return pl.ds(pl.multiple_of(which * share, share), share)

    def as_rank(me):
        peers = [(me + k) % ranks for k in range(1, ranks)]

        def send_share(peer, c):
            return pltpu.make_async_remote_copy(
                src_ref=g_own.at[own_share(half), pl.ds(c * wide, wide)],
                dst_ref=g_in.at[me, c, own_share(half)],
                send_sem=g_send.at[peer, c],
                recv_sem=g_recv.at[me, c],
                device_id={"tensor": peer},
                device_id_type=MESH,
            )

        def arrived_share(peer, c):
            place = g_in.at[peer, c, own_share(half)]
            return pltpu.make_async_remote_copy(
                src_ref=place,
                dst_ref=place,
                send_sem=g_send.at[peer, c],
                recv_sem=g_recv.at[peer, c],
                device_id={"tensor": peer},
                device_id_type=MESH,
            )

        def forward(peer, c, which):
            place = g_in.at[peer, c, own_share(which)]
            return pltpu.make_async_remote_copy(
                src_ref=place,
                dst_ref=place,
                send_sem=f_send.at[peer, c],
                recv_sem=f_recv.at[peer, c],
                device_id=partner,
                device_id_type=MESH,
            )

        def to_partner(owner, j):
            return pltpu.make_async_remote_copy(
                src_ref=send1.at[owner, j],
                dst_ref=recv1.at[owner, j],
                send_sem=s1_send.at[owner, j],
                recv_sem=s1_recv.at[owner, j],
                device_id=partner,
                device_id_type=MESH,
            )

        def to_rank(peer, slot, j):
            return pltpu.make_async_remote_copy(
                src_ref=send2.at[peer, j],
                dst_ref=recv2.at[slot, j],
                send_sem=s2_send.at[peer, j],
                recv_sem=s2_recv.at[slot, j],
                device_id={"tensor": peer},
                device_id_type=MESH,
            )

        for c in range(per_rank):
            for peer in peers:
                send_share(peer, c).start()

        @pl.when(jnp.logical_not(first))
        def _():
            shift.start()

        load_x.wait()
        load_counts.wait()
        clear_dead_rows()
        load_m.wait()

        def update(j, gradients):
            cols = pl.ds(j * wide, wide)
            if features == rows:
                x_rows = xt_buf[...]
            else:
                x_rows = xt_buf[pl.ds(me * rows, rows), :]
            grad = jnp.dot(x_rows, gradients, preferred_element_type=jnp.float32)
            grad = grad.astype(jnp.bfloat16).astype(jnp.float32)
            new = (DECAY * m_buf[:, cols].astype(jnp.float32) + grad).astype(jnp.bfloat16)
            new_momentum[:, cols] = new
            if j < ranks:
                nt_buf[j] = new.T

        def piece(owner, j):
            sums = jnp.dot(
                nt_buf[owner],
                new_momentum[:, pl.ds(j * wide, wide)],
                preferred_element_type=jnp.float32,
            )
            top, bottom = sums[:q], sums[q:]
            own[owner, j] = jnp.where(half == 0, top, bottom)
            send1[owner, j] = jnp.where(half == 0, bottom, top).astype(jnp.bfloat16)
            to_partner(owner, j).start()

        def pass_on(owner, j):
            to_partner(owner, j).wait_recv()
            both = own[owner, j] + recv1[owner, j].astype(jnp.float32)
            send2[owner, j] = both.astype(jnp.bfloat16)
            to_rank(owner, me, j).start()

        arrivals = [(peer, c) for c in range(per_rank) for peer in peers]
        coming = list(arrivals)

        def forward_next():
            if coming:
                peer, c = coming.pop(0)
                arrived_share(peer, c).wait_recv()
                forward(peer, c, half).start()

        ready, waiting = [], []

        def pieces(new, forward_after):
            ready.extend(new)
            todo = [
                (owner, j)
                for owner in peers + [me]
                if owner in ready
                for j in (ready if owner in new else new)
            ]
            for n, (owner, j) in enumerate(todo):
                piece(owner, j)
                if n in forward_after:
                    forward_next()
                waiting[:] = [(owner, j, age + 1) for owner, j, age in waiting]
                while waiting and waiting[0][2] >= 2:
                    pass_on(*waiting.pop(0)[:2])
                if owner != me:
                    waiting.append((owner, j, 0))
            return bool(todo)

        mine = [me * per_rank + c for c in range(per_rank)]
        for c in range(per_rank):
            update(mine[c], g_own[:, c * wide:(c + 1) * wide])
        busy = pieces(mine, (1, 3))
        if not busy:
            forward_next()

        @pl.when(last)
        def _():
            received[...] = jnp.zeros_like(received)

        for peer, c in arrivals:
            if (peer, c) in coming:
                forward_next()
            forward(peer, c, 1 - half).wait_recv()
            update(peer * per_rank + c, g_in[peer, c])
            pieces([peer * per_rank + c], (0,))
        while waiting:
            pass_on(*waiting.pop(0)[:2])

        order = ready
        for j in order:
            to_partner(me, j).wait_recv()
            own[me, j] = own[me, j] + recv1[me, j].astype(jnp.float32)
        for j in order[per_rank:] + order[:per_rank]:
            total = own[me, j]
            for peer in peers:
                to_rank(peer, peer, j).wait_recv()
                total = total + recv2[peer, j].astype(jnp.float32)
            gram[:, pl.ds(j * wide, wide)] = total / D

        for peer, c in arrivals:
            send_share(peer, c).wait_send()
            forward(peer, c, half).wait_send()
        for j in order:
            for owner in peers + [me]:
                to_partner(owner, j).wait_send()
            for peer in peers:
                to_rank(peer, me, j).wait_send()

    for me in range(ranks):

        @pl.when(rank == me)
        def _():
            as_rank(me)

    @pl.when(jnp.logical_not(first))
    def _():
        shift.wait_send()

    @pl.when(jnp.logical_not(last))
    def _():
        shift.wait_recv()


def write_out(cuts, *refs):
    count = len(cuts)
    sems = refs[-1]
    copies = []
    for i, cut in enumerate(cuts):
        rows = refs[i].shape[-2] // cut
        for n in range(cut):
            place = (slice(None),) * (len(refs[i].shape) - 2) + (pl.ds(n * rows, rows),)
            copies.append(
                pltpu.make_async_copy(
                    refs[i].at[place], refs[count + i].at[place], sems.at[len(copies)]
                )
            )
    for copy in copies:
        copy.start()
    for copy in copies:
        copy.wait()


def on_device(acts, hidden_grad, counts, momentum, act_grad):
    sections, ranks = lax.axis_size("pipe"), lax.axis_size("tensor")
    row_count, features = acts.shape[2:]
    rows, units = momentum.shape[2:]
    width = hidden_grad.shape[3]
    q = PANEL // (2 * ranks)
    wide = 2 * q
    blocks = units // wide
    x_cols = rows if rows % 128 == 0 else features
    bf16, f32 = jnp.bfloat16, jnp.float32
    vmem, dma = pltpu.VMEM, pltpu.SemaphoreType.DMA
    hbm = pl.BlockSpec(memory_space=pltpu.HBM)
    anywhere = pl.BlockSpec(memory_space=pl.ANY)
    in_vmem = pl.BlockSpec(memory_space=vmem)

    def keep(x):
        return pltpu.with_memory_space_constraint(x, pltpu.HBM)

    results = pl.pallas_call(
        functools.partial(kernel, sections, ranks),
        out_shape=(
            vmem((rows, units), bf16),
            vmem((q, units), f32),
            vmem(act_grad.shape, bf16),
        ),
        in_specs=[hbm] * 5,
        out_specs=(in_vmem, in_vmem, in_vmem),
        scratch_shapes=[
            pltpu.SMEM(counts.shape, counts.dtype),
            vmem((row_count, x_cols), bf16),
            vmem((row_count, width), bf16),
            vmem((rows, units), bf16),
            vmem((x_cols, row_count), bf16),
            vmem((ranks, width // wide, row_count, wide), bf16),
            vmem((ranks, wide, rows), bf16),
            vmem((ranks, blocks, q, wide), f32),
            vmem((ranks, blocks, q, wide), bf16),
            vmem((ranks, blocks, q, wide), bf16),
            vmem((ranks, blocks, q, wide), bf16),
            vmem((ranks, blocks, q, wide), bf16),
            dma((4,)), dma, dma,
            dma((ranks, width // wide)), dma((ranks, width // wide)),
            dma((ranks, width // wide)), dma((ranks, width // wide)),
            dma((ranks, blocks)), dma((ranks, blocks)),
            dma((ranks, blocks)), dma((ranks, blocks)),
        ],
        compiler_params=pltpu.CompilerParams(
            collective_id=0, has_side_effects=True, vmem_limit_bytes=32 * 2**20
        ),
    )(keep(acts), keep(hidden_grad), keep(counts), keep(momentum), keep(act_grad))
    new_momentum, gram, received = pl.pallas_call(
        functools.partial(write_out, (4, 2, 2)),
        out_shape=tuple(pltpu.HBM(r.shape, r.dtype) for r in results),
        in_specs=[in_vmem] * 3,
        out_specs=(hbm,) * 3,
        scratch_shapes=[dma((8,))],
    )(*[pltpu.with_memory_space_constraint(r, vmem) for r in results])
    return (new_momentum[None, None], gram[None, None], received)


def solution(mesh):
    return jax.shard_map(
        on_device,
        mesh=mesh,
        in_specs=(
            P("pipe", "expert", None, None),
            P("pipe", None, None, "tensor"),
            P("pipe", None, None),
            P("pipe", "expert", "tensor", None),
            P("pipe", "expert", "tensor"),
        ),
        out_specs=(
            P("pipe", "expert", "tensor", None),
            P("pipe", "expert", "tensor", None),
            P("pipe", "expert", "tensor"),
        ),
        check_vma=False,
    )
```

profile of v0, /device:TPU:0, one launch (start us, length us, event | category | flops | bytes accessed | tf_op | source)
XLA Modules:
  0.0 19.6 jit_solution(1019512480034307848)
XLA Ops:
  0.6 17.4 %shard_map.76 = (bf16[896,1024]{1,0:T(8,128)(2,1)S(1)}, f32[128,1024]{1,0:T(8,128)S(1)}, bf16[1,64,3584]{2,1,0:T(8,128)(2,1)S(1)}) custom-call(bf16[1,1,256,1792]{3,2,1,0:T(8,128)(2,1)} %acts.1, bf16[1,2,256,512]{3,2,1,0:T(8,128)(2,1)} %hidden.1, s32[1,2,2]{2,1,0:T(2,128)} %counts_in.1, bf16[1,1,896,1024]{3,2,1,0:T(8,128)(2,1)} %momentum.1, ...), custom_call_target="tpu_custom_call" | custom-call | tf_op jit(solution)/shard_map/pallas_call | solution.py:313
  18.0 1.6 %shard_map.77 = (bf16[896,1024]{1,0:T(8,128)(2,1)}, f32[128,1024]{1,0:T(8,128)}, bf16[1,64,3584]{2,1,0:T(8,128)(2,1)}) custom-call(bf16[896,1024]{1,0:T(8,128)(2,1)S(1)} %get-tuple-element.9.refs_0_, f32[128,1024]{1,0:T(8,128)S(1)} %get-tuple-element.10.refs_1_, bf16[1,64,3584]{2,1,0:T(8,128)(2,1)S(1)} %get-tuple-element.11.refs_2_), custom_call_target="tpu_custom_call" | custom-call | tf_op jit(solution)/shard_map/pallas_call | solution.py:345
where the time goes:
time: 19.8 us; the launch traced here: 19.6 us
  Pallas kernels  19 us (96%)
  between operations  0.64 us (3%)
    pallas_call x1, Pallas kernels, on_device(): pl.pallas_call(functools.partial(kernel, sections, ranks), out_shape=(vme...  17.4 us
    pallas_call x1, Pallas kernels, on_device(): pl.pallas_call(functools.partial(write_out, (4, 2, 2)), out_shape=tuple((...  1.61 us

commit v1 on v0

--- a/solution.py
+++ b/solution.py
@@ -19,19 +19,22 @@
     new_momentum, gram, received,
     counts, x_buf, g_own, m_buf, xt_buf, g_in, nt_buf, own, send1, recv1, send2, recv2,
     load_sem, shift_send, shift_recv,
-    g_send, g_recv, f_send, f_recv, s1_send, s1_recv, s2_send, s2_recv,
+    d_send, d_recv, g_send, g_recv, f_send, f_recv, s1_send, s1_recv, s2_send, s2_recv,
 ):
     section = lax.axis_index("pipe")
     expert_rank = lax.axis_index("expert")
     rank = lax.axis_index("tensor")
     pair = expert_rank // 2
     half = expert_rank % 2
-    partner = {"expert": expert_rank + 1 - 2 * half}
+    other_half = expert_rank + 1 - 2 * half
+    partner = {"expert": other_half}
     row_count, features = x_buf.shape
     rows, hidden_units = new_momentum.shape
     q, wide = send1.shape[2:]
     per_rank = g_own.shape[1] // wide
     share = row_count // 2
+    subs = 2 if q % 128 == 0 else 1
+    thin = wide // subs
     first, last = section == 0, section == sections - 1
 
     if features == rows:
@@ -50,6 +53,12 @@
         pl.semaphore_signal(
             barrier, inc=1, device_id={"tensor": (rank + k) % ranks}, device_id_type=MESH
         )
+        pl.semaphore_signal(
+            barrier,
+            inc=1,
+            device_id={"expert": other_half, "tensor": (rank + k) % ranks},
+            device_id_type=MESH,
+        )
 
     @pl.when(jnp.logical_not(first))
     def _():
@@ -64,7 +73,7 @@
     load_counts.start()
     load_m.start()
     load_g.wait()
-    pl.semaphore_wait(barrier, ranks + 2 - ends)
+    pl.semaphore_wait(barrier, 2 * ranks + 1 - ends)
 
     shift = pltpu.make_async_remote_copy(
         src_ref=act_grad,
@@ -125,6 +134,35 @@
                 device_id_type=MESH,
             )
 
+        def direct(peer, c):
+            return c == 0 and peer * per_rank < ranks
+
+        def send_direct(peer, away, sub):
+            target = {"tensor": peer}
+            if away:
+                target["expert"] = other_half
+            cols = pl.ds(sub * thin, thin)
+            return pltpu.make_async_remote_copy(
+                src_ref=g_own.at[own_share(half), cols],
+                dst_ref=g_in.at[me, 0, own_share(half), cols],
+                send_sem=d_send.at[peer, away, sub],
+                recv_sem=d_recv.at[me, away, sub],
+                device_id=target,
+                device_id_type=MESH,
+            )
+
+        def arrived_direct(peer, away, sub):
+            which = 1 - half if away else half
+            place = g_in.at[peer, 0, own_share(which), pl.ds(sub * thin, thin)]
+            return pltpu.make_async_remote_copy(
+                src_ref=place,
+                dst_ref=place,
+                send_sem=d_send.at[peer, away, sub],
+                recv_sem=d_recv.at[peer, away, sub],
+                device_id={"tensor": peer},
+                device_id_type=MESH,
+            )
+
         def to_partner(owner, j):
             return pltpu.make_async_remote_copy(
                 src_ref=send1.at[owner, j],
@@ -146,8 +184,14 @@
             )
 
         for c in range(per_rank):
-            for peer in peers:
-                send_share(peer, c).start()
+            if direct(me, c):
+                for sub in range(subs):
+                    for peer in peers:
+                        for away in range(2):
+                            send_direct(peer, away, sub).start()
+            else:
+                for peer in peers:
+                    send_share(peer, c).start()
 
         @pl.when(jnp.logical_not(first))
         def _():
@@ -158,8 +202,9 @@
         clear_dead_rows()
         load_m.wait()
 
-        def update(j, gradients):
-            cols = pl.ds(j * wide, wide)
+        def update(j, gradients, at=0):
+            size = gradients.shape[1]
+            cols = pl.ds(j * wide + at, size)
             if features == rows:
                 x_rows = xt_buf[...]
             else:
@@ -169,7 +214,7 @@
             new = (DECAY * m_buf[:, cols].astype(jnp.float32) + grad).astype(jnp.bfloat16)
             new_momentum[:, cols] = new
             if j < ranks:
-                nt_buf[j] = new.T
+                nt_buf[j, pl.ds(at, size)] = new.T
 
         def piece(owner, j):
             sums = jnp.dot(
@@ -182,6 +227,22 @@
             send1[owner, j] = jnp.where(half == 0, bottom, top).astype(jnp.bfloat16)
             to_partner(owner, j).start()
 
+        def half_piece(owner, j, keeper):
+            sums = jnp.dot(
+                nt_buf[owner, pl.ds(keeper * q, q)],
+                new_momentum[:, pl.ds(j * wide, wide)],
+                preferred_element_type=jnp.float32,
+            )
+
+            @pl.when(half == keeper)
+            def _():
+                own[owner, j] = sums
+
+            @pl.when(half != keeper)
+            def _():
+                send1[owner, j] = sums.astype(jnp.bfloat16)
+                to_partner(owner, j).start()
+
         def pass_on(owner, j):
             to_partner(owner, j).wait_recv()
             both = own[owner, j] + recv1[owner, j].astype(jnp.float32)
@@ -189,7 +250,7 @@
             to_rank(owner, me, j).start()
 
         arrivals = [(peer, c) for c in range(per_rank) for peer in peers]
-        coming = list(arrivals)
+        coming = [a for a in arrivals if not direct(*a)]
 
         def forward_next():
             if coming:
@@ -199,13 +260,14 @@
 
         ready, waiting = [], []
 
-        def pieces(new, forward_after):
+        def pieces(new, forward_after, done=()):
             ready.extend(new)
             todo = [
                 (owner, j)
                 for owner in peers + [me]
                 if owner in ready
                 for j in (ready if owner in new else new)
+                if (owner, j) not in done
             ]
             for n, (owner, j) in enumerate(todo):
                 piece(owner, j)
@@ -216,25 +278,49 @@
                     pass_on(*waiting.pop(0)[:2])
                 if owner != me:
                     waiting.append((owner, j, 0))
-            return bool(todo)
 
         mine = [me * per_rank + c for c in range(per_rank)]
         for c in range(per_rank):
             update(mine[c], g_own[:, c * wide:(c + 1) * wide])
-        busy = pieces(mine, (1, 3))
-        if not busy:
-            forward_next()
+        pieces(mine, (1, 3))
 
         @pl.when(last)
         def _():
             received[...] = jnp.zeros_like(received)
 
         for peer, c in arrivals:
+            j = peer * per_rank + c
+            if direct(peer, c):
+                before = list(ready)
+                for sub in range(subs):
+                    for away in range(2):
+                        arrived_direct(peer, away, sub).wait_recv()
+                    update(j, g_in[peer, c, :, pl.ds(sub * thin, thin)], sub * thin)
+                    if subs == 2:
+                        for i in before:
+                            half_piece(j, i, sub)
+                done = [(j, i) for i in before] if subs == 2 else []
+                if done and j != me:
+
+                    @pl.when(half == 0)
+                    def _():
+                        for item in done:
+                            pass_on(*item)
+
+                pieces([j], (0,), done)
+                if done and j != me:
+
+                    @pl.when(half == 1)
+                    def _():
+                        for item in done:
+                            pass_on(*item)
+
+                continue
             if (peer, c) in coming:
                 forward_next()
             forward(peer, c, 1 - half).wait_recv()
-            update(peer * per_rank + c, g_in[peer, c])
-            pieces([peer * per_rank + c], (0,))
+            update(j, g_in[peer, c])
+            pieces([j], (0,))
         while waiting:
             pass_on(*waiting.pop(0)[:2])
 
@@ -250,8 +336,14 @@
             gram[:, pl.ds(j * wide, wide)] = total / D
 
         for peer, c in arrivals:
-            send_share(peer, c).wait_send()
-            forward(peer, c, half).wait_send()
+            if direct(me, c):
+                for sub in range(subs):
+                    for away in range(2):
+                        send_direct(peer, away, sub).wait_send()
+            else:
+                send_share(peer, c).wait_send()
+            if not direct(peer, c):
+                forward(peer, c, half).wait_send()
         for j in order:
             for owner in peers + [me]:
                 to_partner(owner, j).wait_send()
@@ -333,6 +425,7 @@
             vmem((ranks, blocks, q, wide), bf16),
             vmem((ranks, blocks, q, wide), bf16),
             dma((4,)), dma, dma,
+            dma((ranks, 2, 2)), dma((ranks, 2, 2)),
             dma((ranks, width // wide)), dma((ranks, width // wide)),
             dma((ranks, width // wide)), dma((ranks, width // wide)),
             dma((ranks, blocks)), dma((ranks, blocks)),

time: 19.8 us -> 19.8 us (level)
  no operation moved by 1% of the time
where the time goes in v1:
time: 19.8 us; the launch traced here: 19.7 us
  Pallas kernels  19 us (96%)
  between operations  0.64 us (3%)
    pallas_call x1, Pallas kernels, on_device(): pl.pallas_call(functools.partial(kernel, sections, ranks), out_shape=(vme...  17.4 us
    pallas_call x1, Pallas kernels, on_device(): pl.pallas_call(functools.partial(write_out, (4, 2, 2)), out_shape=tuple((...  1.61 us

profile of v1, /device:TPU:0, one launch (start us, length us, event | category | flops | bytes accessed | tf_op | source)
XLA Modules:
  0.0 19.7 jit_solution(17128375636708695976)
XLA Ops:
  0.6 17.4 %shard_map.76 = (bf16[896,1024]{1,0:T(8,128)(2,1)S(1)}, f32[128,1024]{1,0:T(8,128)S(1)}, bf16[1,64,3584]{2,1,0:T(8,128)(2,1)S(1)}) custom-call(bf16[1,1,256,1792]{3,2,1,0:T(8,128)(2,1)} %acts.1, bf16[1,2,256,512]{3,2,1,0:T(8,128)(2,1)} %hidden.1, s32[1,2,2]{2,1,0:T(2,128)} %counts_in.1, bf16[1,1,896,1024]{3,2,1,0:T(8,128)(2,1)} %momentum.1, ...), custom_call_target="tpu_custom_call" | custom-call | tf_op jit(solution)/shard_map/pallas_call | solution.py:405
  18.1 1.6 %shard_map.77 = (bf16[896,1024]{1,0:T(8,128)(2,1)}, f32[128,1024]{1,0:T(8,128)}, bf16[1,64,3584]{2,1,0:T(8,128)(2,1)}) custom-call(bf16[896,1024]{1,0:T(8,128)(2,1)S(1)} %get-tuple-element.9.refs_0_, f32[128,1024]{1,0:T(8,128)S(1)} %get-tuple-element.10.refs_1_, bf16[1,64,3584]{2,1,0:T(8,128)(2,1)S(1)} %get-tuple-element.11.refs_2_), custom_call_target="tpu_custom_call" | custom-call | tf_op jit(solution)/shard_map/pallas_call | solution.py:438

commit v2 on v1

--- a/solution.py
+++ b/solution.py
@@ -202,6 +202,8 @@
         clear_dead_rows()
         load_m.wait()
 
+        flipped = set()
+
         def update(j, gradients, at=0):
             size = gradients.shape[1]
             cols = pl.ds(j * wide + at, size)
@@ -213,10 +215,14 @@
             grad = grad.astype(jnp.bfloat16).astype(jnp.float32)
             new = (DECAY * m_buf[:, cols].astype(jnp.float32) + grad).astype(jnp.bfloat16)
             new_momentum[:, cols] = new
-            if j < ranks:
+            if at or size < wide:
                 nt_buf[j, pl.ds(at, size)] = new.T
+                flipped.add(j)
 
         def piece(owner, j):
+            if owner not in flipped:
+                nt_buf[owner] = new_momentum[:, pl.ds(owner * wide, wide)].T
+                flipped.add(owner)
             sums = jnp.dot(
                 nt_buf[owner],
                 new_momentum[:, pl.ds(j * wide, wide)],
@@ -318,6 +324,8 @@
                 continue
             if (peer, c) in coming:
                 forward_next()
+            while waiting:
+                pass_on(*waiting.pop(0)[:2])
             forward(peer, c, 1 - half).wait_recv()
             update(j, g_in[peer, c])
             pieces([j], (0,))

time: 19.8 us -> 19.5 us (0.985)
  Pallas kernels: 19 us -> 18.7 us
    pallas_call x1, Pallas kernels: 17.4 us -> 17.1 us  [on_device(): pl.pallas_call(functools.partial(kernel, sections, ranks), out_shape=(vme...]
where the time goes in v2:
time: 19.5 us; the launch traced here: 19.4 us
  Pallas kernels  18.7 us (96%)
  between operations  0.64 us (3%)
    pallas_call x1, Pallas kernels, on_device(): pl.pallas_call(functools.partial(kernel, sections, ranks), out_shape=(vme...  17.1 us
    pallas_call x1, Pallas kernels, on_device(): pl.pallas_call(functools.partial(write_out, (4, 2, 2)), out_shape=tuple((...  1.61 us

profile of v2, /device:TPU:0, one launch (start us, length us, event | category | flops | bytes accessed | tf_op | source)
XLA Modules:
  0.0 19.4 jit_solution(16263282830542859629)
XLA Ops:
  0.6 17.1 %shard_map.76 = (bf16[896,1024]{1,0:T(8,128)(2,1)S(1)}, f32[128,1024]{1,0:T(8,128)S(1)}, bf16[1,64,3584]{2,1,0:T(8,128)(2,1)S(1)}) custom-call(bf16[1,1,256,1792]{3,2,1,0:T(8,128)(2,1)} %acts.1, bf16[1,2,256,512]{3,2,1,0:T(8,128)(2,1)} %hidden.1, s32[1,2,2]{2,1,0:T(2,128)} %counts_in.1, bf16[1,1,896,1024]{3,2,1,0:T(8,128)(2,1)} %momentum.1, ...), custom_call_target="tpu_custom_call" | custom-call | tf_op jit(solution)/shard_map/pallas_call | solution.py:413
  17.7 1.6 %shard_map.77 = (bf16[896,1024]{1,0:T(8,128)(2,1)}, f32[128,1024]{1,0:T(8,128)}, bf16[1,64,3584]{2,1,0:T(8,128)(2,1)}) custom-call(bf16[896,1024]{1,0:T(8,128)(2,1)S(1)} %get-tuple-element.9.refs_0_, f32[128,1024]{1,0:T(8,128)S(1)} %get-tuple-element.10.refs_1_, bf16[1,64,3584]{2,1,0:T(8,128)(2,1)S(1)} %get-tuple-element.11.refs_2_), custom_call_target="tpu_custom_call" | custom-call | tf_op jit(solution)/shard_map/pallas_call | solution.py:446

commit v3 on v0

--- a/solution.py
+++ b/solution.py
@@ -158,6 +158,8 @@
         clear_dead_rows()
         load_m.wait()
 
+        flipped = set()
+
         def update(j, gradients):
             cols = pl.ds(j * wide, wide)
             if features == rows:
@@ -168,10 +170,11 @@
             grad = grad.astype(jnp.bfloat16).astype(jnp.float32)
             new = (DECAY * m_buf[:, cols].astype(jnp.float32) + grad).astype(jnp.bfloat16)
             new_momentum[:, cols] = new
-            if j < ranks:
-                nt_buf[j] = new.T
 
         def piece(owner, j):
+            if owner not in flipped:
+                nt_buf[owner] = new_momentum[:, pl.ds(owner * wide, wide)].T
+                flipped.add(owner)
             sums = jnp.dot(
                 nt_buf[owner],
                 new_momentum[:, pl.ds(j * wide, wide)],
@@ -199,7 +202,7 @@
 
         ready, waiting = [], []
 
-        def pieces(new, forward_after):
+        def pieces(new, forward_after=()):
             ready.extend(new)
             todo = [
                 (owner, j)
@@ -212,29 +215,30 @@
                 if n in forward_after:
                     forward_next()
                 waiting[:] = [(owner, j, age + 1) for owner, j, age in waiting]
-                while waiting and waiting[0][2] >= 2:
+                while waiting and (waiting[0][2] >= 2 or n == 0):
                     pass_on(*waiting.pop(0)[:2])
                 if owner != me:
                     waiting.append((owner, j, 0))
-            return bool(todo)
 
         mine = [me * per_rank + c for c in range(per_rank)]
         for c in range(per_rank):
             update(mine[c], g_own[:, c * wide:(c + 1) * wide])
-        busy = pieces(mine, (1, 3))
-        if not busy:
-            forward_next()
+            if c == 0:
+                forward_next()
+        pieces(mine, (1,))
 
         @pl.when(last)
         def _():
             received[...] = jnp.zeros_like(received)
 
         for peer, c in arrivals:
+            j = peer * per_rank + c
             if (peer, c) in coming:
                 forward_next()
             forward(peer, c, 1 - half).wait_recv()
-            update(peer * per_rank + c, g_in[peer, c])
-            pieces([peer * per_rank + c], (0,))
+            forward_next()
+            update(j, g_in[peer, c])
+            pieces([j])
         while waiting:
             pass_on(*waiting.pop(0)[:2])
 

time: 19.8 us -> 19.8 us (level)
  no operation moved by 1% of the time
where the time goes in v3:
time: 19.8 us; the launch traced here: 19.6 us
  Pallas kernels  19 us (96%)
  between operations  0.64 us (3%)
    pallas_call x1, Pallas kernels, on_device(): pl.pallas_call(functools.partial(kernel, sections, ranks), out_shape=(vme...  17.4 us
    pallas_call x1, Pallas kernels, on_device(): pl.pallas_call(functools.partial(write_out, (4, 2, 2)), out_shape=tuple((...  1.61 us

profile of v3, /device:TPU:0, one launch (start us, length us, event | category | flops | bytes accessed | tf_op | source)
XLA Modules:
  0.0 19.6 jit_solution(16893068327220966583)
XLA Ops:
  0.6 17.4 %shard_map.76 = (bf16[896,1024]{1,0:T(8,128)(2,1)S(1)}, f32[128,1024]{1,0:T(8,128)S(1)}, bf16[1,64,3584]{2,1,0:T(8,128)(2,1)S(1)}) custom-call(bf16[1,1,256,1792]{3,2,1,0:T(8,128)(2,1)} %acts.1, bf16[1,2,256,512]{3,2,1,0:T(8,128)(2,1)} %hidden.1, s32[1,2,2]{2,1,0:T(2,128)} %counts_in.1, bf16[1,1,896,1024]{3,2,1,0:T(8,128)(2,1)} %momentum.1, ...), custom_call_target="tpu_custom_call" | custom-call | tf_op jit(solution)/shard_map/pallas_call | solution.py:317
  18.0 1.6 %shard_map.77 = (bf16[896,1024]{1,0:T(8,128)(2,1)}, f32[128,1024]{1,0:T(8,128)}, bf16[1,64,3584]{2,1,0:T(8,128)(2,1)}) custom-call(bf16[896,1024]{1,0:T(8,128)(2,1)S(1)} %get-tuple-element.9.refs_0_, f32[128,1024]{1,0:T(8,128)S(1)} %get-tuple-element.10.refs_1_, bf16[1,64,3584]{2,1,0:T(8,128)(2,1)S(1)} %get-tuple-element.11.refs_2_), custom_call_target="tpu_custom_call" | custom-call | tf_op jit(solution)/shard_map/pallas_call | solution.py:349

commit v4 on v2

--- a/solution.py
+++ b/solution.py
@@ -233,21 +233,23 @@
             send1[owner, j] = jnp.where(half == 0, bottom, top).astype(jnp.bfloat16)
             to_partner(owner, j).start()
 
-        def half_piece(owner, j, keeper):
+        def half_pieces(owner, start, count, keeper):
             sums = jnp.dot(
                 nt_buf[owner, pl.ds(keeper * q, q)],
-                new_momentum[:, pl.ds(j * wide, wide)],
+                new_momentum[:, pl.ds(start * wide, count * wide)],
                 preferred_element_type=jnp.float32,
             )
 
             @pl.when(half == keeper)
             def _():
-                own[owner, j] = sums
+                for n in range(count):
+                    own[owner, start + n] = sums[:, n * wide:(n + 1) * wide]
 
             @pl.when(half != keeper)
             def _():
-                send1[owner, j] = sums.astype(jnp.bfloat16)
-                to_partner(owner, j).start()
+                for n in range(count):
+                    send1[owner, start + n] = sums[:, n * wide:(n + 1) * wide].astype(jnp.bfloat16)
+                    to_partner(owner, start + n).start()
 
         def pass_on(owner, j):
             to_partner(owner, j).wait_recv()
@@ -303,8 +305,8 @@
                         arrived_direct(peer, away, sub).wait_recv()
                     update(j, g_in[peer, c, :, pl.ds(sub * thin, thin)], sub * thin)
                     if subs == 2:
-                        for i in before:
-                            half_piece(j, i, sub)
+                        for i in before[::per_rank]:
+                            half_pieces(j, i, per_rank, sub)
                 done = [(j, i) for i in before] if subs == 2 else []
                 if done and j != me:
 

time: 19.5 us -> 19.5 us (level)
  no operation moved by 1% of the time
where the time goes in v4:
time: 19.5 us; the launch traced here: 19.4 us
  Pallas kernels  18.7 us (96%)
  between operations  0.64 us (3%)
    pallas_call x1, Pallas kernels, on_device(): pl.pallas_call(functools.partial(kernel, sections, ranks), out_shape=(vme...  17.1 us
    pallas_call x1, Pallas kernels, on_device(): pl.pallas_call(functools.partial(write_out, (4, 2, 2)), out_shape=tuple((...  1.61 us

profile of v4, /device:TPU:0, one launch (start us, length us, event | category | flops | bytes accessed | tf_op | source)
XLA Modules:
  0.0 19.4 jit_solution(14596868407185267360)
XLA Ops:
  0.6 17.1 %shard_map.76 = (bf16[896,1024]{1,0:T(8,128)(2,1)S(1)}, f32[128,1024]{1,0:T(8,128)S(1)}, bf16[1,64,3584]{2,1,0:T(8,128)(2,1)S(1)}) custom-call(bf16[1,1,256,1792]{3,2,1,0:T(8,128)(2,1)} %acts.1, bf16[1,2,256,512]{3,2,1,0:T(8,128)(2,1)} %hidden.1, s32[1,2,2]{2,1,0:T(2,128)} %counts_in.1, bf16[1,1,896,1024]{3,2,1,0:T(8,128)(2,1)} %momentum.1, ...), custom_call_target="tpu_custom_call" | custom-call | tf_op jit(solution)/shard_map/pallas_call | solution.py:415
  17.7 1.6 %shard_map.77 = (bf16[896,1024]{1,0:T(8,128)(2,1)}, f32[128,1024]{1,0:T(8,128)}, bf16[1,64,3584]{2,1,0:T(8,128)(2,1)}) custom-call(bf16[896,1024]{1,0:T(8,128)(2,1)S(1)} %get-tuple-element.9.refs_0_, f32[128,1024]{1,0:T(8,128)S(1)} %get-tuple-element.10.refs_1_, bf16[1,64,3584]{2,1,0:T(8,128)(2,1)S(1)} %get-tuple-element.11.refs_2_), custom_call_target="tpu_custom_call" | custom-call | tf_op jit(solution)/shard_map/pallas_call | solution.py:448
